TPU v7x, 32 devices: a whole 2x2x4 slice. The times are simulated.
32 devices in a mesh: dp: 4 (over y, x), seq: 8 (over z, core).
Axes of the slice: x: 2, y: 2, z: 4, core: 2. Of those that a mesh axis runs over, the one named last changes fastest.
Arguments:
- inputs: bfloat16 [8, 1024, 768], P('dp', 'seq'), may hold values from -6 to 6
- memory: bfloat16 [8, 1024, 768], P('dp', 'seq'), may hold values from -6 to 6
- cotangent: bfloat16 [8, 1024, 768], P('dp', 'seq'), may hold values from -6 to 6
- segment_ids: int32 [8, 1024], P('dp', 'seq'), may hold values from 0 to 3, never falling along the last dimension, each value on 1 to 512 neighbouring positions
- row_live: int32 [8], P('dp'), may hold values 0 or 1
- buckets: int32 [1024], replicated, may hold values from 0 to 31, as said below
- gain_self: bfloat16 [768], P('dp'), may hold values from 0.5 to 1.5
- w_qkv: bfloat16 [768, 2304], P('dp'), may hold values from -0.21875 to 0.21875
- w_attn_out: bfloat16 [768, 768], P('dp'), may hold values from -2 to 2
- rel_bias: bfloat16 [32, 12], P('dp'), may hold values from -4 to 4
- gain_cross: bfloat16 [768], P('dp'), may hold values from 0.5 to 1.5
- c_query: bfloat16 [768, 768], P('dp'), may hold values from -0.21875 to 0.21875
- c_keyval: bfloat16 [768, 1536], P('dp'), may hold values from -0.21875 to 0.21875
- c_out: bfloat16 [768, 768], P('dp'), may hold values from -2 to 2
- gain_ff: bfloat16 [768], P('dp'), may hold values from 0.5 to 1.5
- w_gate_up: bfloat16 [768, 4096], P('dp'), may hold values from -0.21875 to 0.21875
- w_down: bfloat16 [2048, 768], P('dp'), may hold values from -0.125 to 0.125
Outputs:
- output: bfloat16 [8, 1024, 768], P('dp', 'seq')
- grad_inputs: bfloat16 [8, 1024, 768], P('dp', 'seq')
- grad_memory: bfloat16 [8, 1024, 768], P('dp', 'seq')
- grad_gain_self: float32 [768], P('dp')
- grad_w_qkv: float32 [768, 2304], P('dp')
- grad_w_attn_out: float32 [768, 768], P('dp')
- grad_rel_bias: float32 [32, 12], P('dp')
- grad_gain_cross: float32 [768], P('dp')
- grad_c_query: float32 [768, 768], P('dp')
- grad_c_keyval: float32 [768, 1536], P('dp')
- grad_c_out: float32 [768, 768], P('dp')
- grad_gain_ff: float32 [768], P('dp')
- grad_w_gate_up: float32 [768, 4096], P('dp')
- grad_w_down: float32 [2048, 768], P('dp')
Inputs may be any that keep to these rules, and one draw needn't show every extreme that they name: `segment_ids`: along each row the segment ids never fall; every row holds all 4 segments. buckets[d] never falls as the distance d grows, is 0 at d = 0 and reaches 31.
All inputs are finite; a program needn't handle non-finite values. No bound on the sum of `row_live` on one device may be relied on, other than what follows from the above.
Results may differ from a plain program's by a relative error of at most 0.029.
Values may be sent and summed in bfloat16 or wider, within the bound.
A program may use at most 192 MiB of HBM per device.

v0:
```python
import jax
import jax.numpy as jnp
from jax import lax
from jax.experimental import pallas as pl
from jax.experimental.pallas import tpu as pltpu
from jax.sharding import PartitionSpec as P

D = 768
HEADS = 12
HEAD_DIM = 64
FF = 2048
BUCKETS = 32
LEN = 1024
MEM = 1024


epsilon = 1e-06
masked_score = -1000000000.0
highest = lax.Precision.HIGHEST


def rms_norm(values, gain):
    return values * lax.rsqrt(jnp.mean(values * values, axis=-1, keepdims=True) + epsilon) * gain


def matmul(left, right, form):
    return jnp.einsum(form, left, right, preferred_element_type=jnp.float32)


def softmax_parts(scores):
    top = jnp.max(scores, axis=-1, keepdims=True)
    expo = jnp.exp(scores - top)
    total = jnp.sum(expo, axis=-1, keepdims=True)
    return (expo / total, (top + jnp.log(total))[..., 0])


def score_grads(scores, lse_row, value_row, grad_row):
    probs = jnp.exp(scores - lse_row[..., None])
    grad_probs = matmul(grad_row, value_row, "qhd,khd->hqk")
    centre = jnp.sum(grad_probs * probs, axis=-1, keepdims=True)
    grad_scores = (probs * (grad_probs - centre)).astype(jnp.bfloat16)
    return (probs, grad_scores, centre[..., 0])


def one_hot_of(buckets):
    return (buckets[:, None] == jnp.arange(BUCKETS, dtype=jnp.int32)).astype(jnp.float32)


def skewed(by_dist, start, rows):
    table = jnp.concatenate([jnp.zeros((LEN - 1, HEADS), by_dist.dtype), by_dist], axis=0)
    window = lax.dynamic_slice_in_dim(table, start, rows + LEN - 1, axis=0)
    line = jnp.pad(window[::-1].T, ((0, 0), (0, 1)))
    width = rows + LEN
    flat = jnp.broadcast_to(line[:, None, :], (HEADS, rows, width)).reshape(HEADS, rows * width)
    return flat[:, : rows * (width - 1)].reshape(HEADS, rows, width - 1)[:, :, rows - 1 :]


def unskewed(block, start, rows):
    width = rows + LEN
    wide = jnp.pad(block, ((0, 0), (0, 0), (rows - 1, 0))).reshape(HEADS, rows * (width - 1))
    line = jnp.sum(jnp.pad(wide, ((0, 0), (0, rows))).reshape(HEADS, rows, width), axis=1)
    window = line[:, : width - 1][:, ::-1].T
    table = jnp.zeros((2 * LEN - 1, HEADS), block.dtype)
    return lax.dynamic_update_slice_in_dim(table, window, start, axis=0)[LEN - 1 :]


def per_device(
    inputs,
    memory,
    cotangent,
    segment_ids,
    row_live,
    buckets,
    gain_self,
    w_qkv,
    w_attn_out,
    rel_bias,
    gain_cross,
    c_query,
    c_keyval,
    c_out,
    gain_ff,
    w_gate_up,
    w_down,
):
    (
        g_self,
        qkv_full,
        out_full,
        bias_full,
        g_cross,
        cq_full,
        ckv_full,
        cout_full,
        g_ffn,
        gu_full,
        down_full,
    ) = (
        lax.all_gather(gain_self, "dp", axis=0, tiled=True),
        lax.all_gather(w_qkv, "dp", axis=0, tiled=True),
        lax.all_gather(w_attn_out, "dp", axis=0, tiled=True),
        lax.all_gather(rel_bias, "dp", axis=0, tiled=True),
        lax.all_gather(gain_cross, "dp", axis=0, tiled=True),
        lax.all_gather(c_query, "dp", axis=0, tiled=True),
        lax.all_gather(c_keyval, "dp", axis=0, tiled=True),
        lax.all_gather(c_out, "dp", axis=0, tiled=True),
        lax.all_gather(gain_ff, "dp", axis=0, tiled=True),
        lax.all_gather(w_gate_up, "dp", axis=0, tiled=True),
        lax.all_gather(w_down, "dp", axis=0, tiled=True),
    )
    num_rows, local_len, _ = inputs.shape
    seq_index = lax.axis_index("seq")
    scale = HEAD_DIM ** (-0.5)
    dense = inputs.astype(jnp.float32)
    live_rows = row_live.astype(jnp.float32)[:, None, None]
    normed_one = rms_norm(dense, g_self.astype(jnp.float32))
    hidden_one = normed_one.astype(jnp.bfloat16)
    qkv_local = matmul(hidden_one, qkv_full, "rcd,de->rce").astype(jnp.bfloat16)
    queries = qkv_local[..., :D]
    key_value = qkv_local[..., D:]
    seg_local = segment_ids.astype(jnp.bfloat16)
    key_all, seg_all = (
        lax.all_gather(key_value, "seq", axis=1, tiled=True),
        lax.all_gather(seg_local, "seq", axis=1, tiled=True),
    )
    positions = seq_index * local_len + jnp.arange(local_len, dtype=jnp.int32)
    offsets = positions[:, None] - jnp.arange(LEN, dtype=jnp.int32)[None, :]
    causal = offsets >= 0
    bucket_hot = one_hot_of(buckets)
    by_dist = jnp.einsum(
        "lb,bh->lh",
        bucket_hot,
        bias_full.astype(jnp.float32),
        precision=highest,
        preferred_element_type=jnp.float32,
    )
    bias_block = skewed(by_dist, seq_index * local_len, local_len)

    def self_scores(queries_h, key_row, seg_row, segk_row):
        raw = matmul(queries_h, key_row, "qhd,khd->hqk") * scale + bias_block
        allowed = causal & (seg_row[:, None] == segk_row[None, :])
        return jnp.where(allowed[None], raw, masked_score)

    def self_forward(items):
        query_row, kv_row, seg_row, segk_row = items
        key_row = kv_row[:, :D].reshape(LEN, HEADS, HEAD_DIM)
        value_row = kv_row[:, D:].reshape(LEN, HEADS, HEAD_DIM)
        scores = self_scores(
            query_row.reshape(local_len, HEADS, HEAD_DIM), key_row, seg_row, segk_row
        )
        probs, lse_row = softmax_parts(scores)
        mixed = matmul(probs.astype(jnp.bfloat16), value_row, "hqk,khd->qhd")
        return (mixed.reshape(local_len, D), lse_row)

    attn_self, lse_self = lax.map(self_forward, (queries, key_all, seg_local, seg_all))
    attn_low = attn_self.astype(jnp.bfloat16)
    branch_one = matmul(attn_low, out_full, "rcd,de->rce")
    after_self = dense + live_rows * branch_one
    normed_two = rms_norm(after_self, g_cross.astype(jnp.float32))
    hidden_two = normed_two.astype(jnp.bfloat16)
    cross_q = matmul(hidden_two, cq_full, "rcd,de->rce").astype(jnp.bfloat16)
    memory_kv = matmul(memory, ckv_full, "rmd,de->rme").astype(jnp.bfloat16)
    memory_all = lax.all_gather(memory_kv, "seq", axis=1, tiled=True)

    def cross_forward(items):
        query_row, kv_row = items
        key_row = kv_row[:, :D].reshape(MEM, HEADS, HEAD_DIM)
        value_row = kv_row[:, D:].reshape(MEM, HEADS, HEAD_DIM)
        scores = (
            matmul(query_row.reshape(local_len, HEADS, HEAD_DIM), key_row, "qhd,khd->hqk") * scale
        )
        probs, lse_row = softmax_parts(scores)
        mixed = matmul(probs.astype(jnp.bfloat16), value_row, "hqk,khd->qhd")
        return (mixed.reshape(local_len, D), lse_row)

    attn_cross, lse_cross = lax.map(cross_forward, (cross_q, memory_all))
    cross_low = attn_cross.astype(jnp.bfloat16)
    branch_two = matmul(cross_low, cout_full, "rcd,de->rce")
    after_cross = after_self + live_rows * branch_two
    normed_three = rms_norm(after_cross, g_ffn.astype(jnp.float32))
    hidden_three = normed_three.astype(jnp.bfloat16)
    gate_up = matmul(hidden_three, gu_full, "rcd,df->rcf")
    gate = gate_up[..., :FF]
    upward = gate_up[..., FF:]
    mixed_ff = (jax.nn.gelu(gate, approximate=True) * upward).astype(jnp.bfloat16)
    branch_three = matmul(mixed_ff, down_full, "rcf,fd->rcd")
    output = (after_cross + live_rows * branch_three).astype(jnp.bfloat16)
    (
        g_self,
        qkv_full,
        out_full,
        bias_full,
        g_cross,
        cq_full,
        ckv_full,
        cout_full,
        g_ffn,
        gu_full,
        down_full,
    ) = (
        lax.all_gather(gain_self, "dp", axis=0, tiled=True),
        lax.all_gather(w_qkv, "dp", axis=0, tiled=True),
        lax.all_gather(w_attn_out, "dp", axis=0, tiled=True),
        lax.all_gather(rel_bias, "dp", axis=0, tiled=True),
        lax.all_gather(gain_cross, "dp", axis=0, tiled=True),
        lax.all_gather(c_query, "dp", axis=0, tiled=True),
        lax.all_gather(c_keyval, "dp", axis=0, tiled=True),
        lax.all_gather(c_out, "dp", axis=0, tiled=True),
        lax.all_gather(gain_ff, "dp", axis=0, tiled=True),
        lax.all_gather(w_gate_up, "dp", axis=0, tiled=True),
        lax.all_gather(w_down, "dp", axis=0, tiled=True),
    )
    grad_out = cotangent.astype(jnp.float32)
    down_in = (live_rows * grad_out).astype(jnp.bfloat16)
    grad_down = matmul(mixed_ff, down_in, "rcf,rcd->fd")
    grad_mixed = matmul(down_in, down_full, "rcd,fd->rcf")
    _, gelu_pull = jax.vjp(
        lambda gate_in, up_in: jax.nn.gelu(gate_in, approximate=True) * up_in, gate, upward
    )
    grad_gate, grad_upward = gelu_pull(grad_mixed)
    grad_gu_low = jnp.concatenate([grad_gate, grad_upward], axis=-1).astype(jnp.bfloat16)
    grad_gate_up = matmul(hidden_three, grad_gu_low, "rcd,rcf->df")
    grad_normed_three = matmul(grad_gu_low, gu_full, "rcf,df->rcd")
    _, pull_three = jax.vjp(rms_norm, after_cross, g_ffn.astype(jnp.float32))
    part_three, grad_gain_ff = pull_three(grad_normed_three)
    grad_after_cross = grad_out + part_three
    cross_in = (live_rows * grad_after_cross).astype(jnp.bfloat16)
    grad_cout = matmul(cross_low, cross_in, "rcd,rce->de")
    grad_cross_attn = matmul(cross_in, cout_full, "rce,de->rcd").astype(jnp.bfloat16)

    def cross_backward(items):
        query_row, kv_row, lse_row, grad_row = items
        queries_h = query_row.reshape(local_len, HEADS, HEAD_DIM)
        grad_h = grad_row.reshape(local_len, HEADS, HEAD_DIM)
        key_row = kv_row[:, :D].reshape(MEM, HEADS, HEAD_DIM)
        value_row = kv_row[:, D:].reshape(MEM, HEADS, HEAD_DIM)
        scores = matmul(queries_h, key_row, "qhd,khd->hqk") * scale
        probs, grad_scores, centre = score_grads(scores, lse_row, value_row, grad_h)
        grad_query = matmul(grad_scores, key_row, "hqk,khd->qhd") * scale
        grad_key = matmul(grad_scores, queries_h, "hqk,qhd->khd") * scale
        grad_value = matmul(probs.astype(jnp.bfloat16), grad_h, "hqk,qhd->khd")
        kv_grads = jnp.concatenate([grad_key.reshape(MEM, D), grad_value.reshape(MEM, D)], axis=-1)
        return (grad_query.reshape(local_len, D), kv_grads, centre)

    grad_cq_rows, grad_memkv_full, _ = lax.map(
        cross_backward, (cross_q, memory_all, lse_cross, grad_cross_attn)
    )
    grad_memkv = lax.psum_scatter(
        grad_memkv_full.astype(jnp.bfloat16), "seq", scatter_dimension=1, tiled=True
    )
    grad_ckv = matmul(memory, grad_memkv, "rmd,rme->de")
    grad_memory = matmul(grad_memkv, ckv_full, "rme,de->rmd").astype(jnp.bfloat16)
    grad_cq_low = grad_cq_rows.astype(jnp.bfloat16)
    grad_cquery = matmul(hidden_two, grad_cq_low, "rcd,rce->de")
    grad_normed_two = matmul(grad_cq_low, cq_full, "rce,de->rcd")
    _, pull_two = jax.vjp(rms_norm, after_self, g_cross.astype(jnp.float32))
    part_two, grad_gain_cross = pull_two(grad_normed_two)
    grad_after_self = grad_after_cross + part_two
    self_in = (live_rows * grad_after_self).astype(jnp.bfloat16)
    grad_wout = matmul(attn_low, self_in, "rcd,rce->de")
    grad_self_attn = matmul(self_in, out_full, "rce,de->rcd").astype(jnp.bfloat16)

    def self_backward(carry, items):
        query_row, kv_row, seg_row, segk_row, lse_row, grad_row = items
        queries_h = query_row.reshape(local_len, HEADS, HEAD_DIM)
        grad_h = grad_row.reshape(local_len, HEADS, HEAD_DIM)
        key_row = kv_row[:, :D].reshape(LEN, HEADS, HEAD_DIM)
        value_row = kv_row[:, D:].reshape(LEN, HEADS, HEAD_DIM)
        scores = self_scores(queries_h, key_row, seg_row, segk_row)
        probs, grad_scores, centre = score_grads(scores, lse_row, value_row, grad_h)
        grad_query = matmul(grad_scores, key_row, "hqk,khd->qhd") * scale
        grad_key = matmul(grad_scores, queries_h, "hqk,qhd->khd") * scale
        grad_value = matmul(probs.astype(jnp.bfloat16), grad_h, "hqk,qhd->khd")
        kv_grads = jnp.concatenate([grad_key.reshape(LEN, D), grad_value.reshape(LEN, D)], axis=-1)
        return (
            carry + grad_scores.astype(jnp.float32),
            (grad_query.reshape(local_len, D), kv_grads, centre),
        )

    zero_block = jnp.zeros((HEADS, local_len, LEN), jnp.float32)
    score_total, (grad_q_rows, grad_kv_full, _) = lax.scan(
        self_backward, zero_block, (queries, key_all, seg_local, seg_all, lse_self, grad_self_attn)
    )
    grad_kv = lax.psum_scatter(
        grad_kv_full.astype(jnp.bfloat16), "seq", scatter_dimension=1, tiled=True
    )
    grad_bias = jnp.einsum(
        "lh,lb->bh",
        unskewed(score_total, seq_index * local_len, local_len),
        bucket_hot,
        precision=highest,
        preferred_element_type=jnp.float32,
    )
    grad_qkv_low = jnp.concatenate([grad_q_rows.astype(jnp.bfloat16), grad_kv], axis=-1)
    grad_wqkv = matmul(hidden_one, grad_qkv_low, "rcd,rce->de")
    grad_normed_one = matmul(grad_qkv_low, qkv_full, "rce,de->rcd")
    _, pull_one = jax.vjp(rms_norm, dense, g_self.astype(jnp.float32))
    part_one, grad_gain_self = pull_one(grad_normed_one)
    grad_inputs = (grad_after_self + part_one).astype(jnp.bfloat16)
    (
        own_gself,
        own_qkv,
        own_wout,
        own_bias,
        own_gcross,
        own_cquery,
        own_ckv,
        own_cout,
        own_gff,
        own_gateup,
        own_down,
    ) = (
        lax.psum_scatter(
            grad_gain_self.astype(jnp.bfloat16), "dp", scatter_dimension=0, tiled=True
        ).astype(jnp.float32),
        lax.psum_scatter(
            grad_wqkv.astype(jnp.bfloat16), "dp", scatter_dimension=0, tiled=True
        ).astype(jnp.float32),
        lax.psum_scatter(
            grad_wout.astype(jnp.bfloat16), "dp", scatter_dimension=0, tiled=True
        ).astype(jnp.float32),
        lax.psum_scatter(
            grad_bias.astype(jnp.bfloat16), "dp", scatter_dimension=0, tiled=True
        ).astype(jnp.float32),
        lax.psum_scatter(
            grad_gain_cross.astype(jnp.bfloat16), "dp", scatter_dimension=0, tiled=True
        ).astype(jnp.float32),
        lax.psum_scatter(
            grad_cquery.astype(jnp.bfloat16), "dp", scatter_dimension=0, tiled=True
        ).astype(jnp.float32),
        lax.psum_scatter(
            grad_ckv.astype(jnp.bfloat16), "dp", scatter_dimension=0, tiled=True
        ).astype(jnp.float32),
        lax.psum_scatter(
            grad_cout.astype(jnp.bfloat16), "dp", scatter_dimension=0, tiled=True
        ).astype(jnp.float32),
        lax.psum_scatter(
            grad_gain_ff.astype(jnp.bfloat16), "dp", scatter_dimension=0, tiled=True
        ).astype(jnp.float32),
        lax.psum_scatter(
            grad_gate_up.astype(jnp.bfloat16), "dp", scatter_dimension=0, tiled=True
        ).astype(jnp.float32),
        lax.psum_scatter(
            grad_down.astype(jnp.bfloat16), "dp", scatter_dimension=0, tiled=True
        ).astype(jnp.float32),
    )
    summed = (
        lax.psum(own_gself.astype(jnp.bfloat16), "seq").astype(jnp.float32),
        lax.psum(own_qkv.astype(jnp.bfloat16), "seq").astype(jnp.float32),
        lax.psum(own_wout.astype(jnp.bfloat16), "seq").astype(jnp.float32),
        lax.psum(own_bias.astype(jnp.bfloat16), "seq").astype(jnp.float32),
        lax.psum(own_gcross.astype(jnp.bfloat16), "seq").astype(jnp.float32),
        lax.psum(own_cquery.astype(jnp.bfloat16), "seq").astype(jnp.float32),
        lax.psum(own_ckv.astype(jnp.bfloat16), "seq").astype(jnp.float32),
        lax.psum(own_cout.astype(jnp.bfloat16), "seq").astype(jnp.float32),
        lax.psum(own_gff.astype(jnp.bfloat16), "seq").astype(jnp.float32),
        lax.psum(own_gateup.astype(jnp.bfloat16), "seq").astype(jnp.float32),
        lax.psum(own_down.astype(jnp.bfloat16), "seq").astype(jnp.float32),
    )
    return (
        output,
        grad_inputs,
        grad_memory,
        summed[0],
        summed[1],
        summed[2],
        summed[3],
        summed[4],
        summed[5],
        summed[6],
        summed[7],
        summed[8],
        summed[9],
        summed[10],
    )


f32, bf16 = jnp.float32, jnp.bfloat16
BIG = 1.0e9
SCALE = HEAD_DIM ** (-0.5)
MESH = pl.DeviceIdType.MESH
GELU_A, GELU_B = 0.7978845608028654, 0.044715
N_SEM, N_LOCAL = 232, 32


def flip(v, k, bits):
    for i in range(bits):
        if (k >> i) & 1:
            b = 1 << i
            v = v + b - 2 * b * lax.rem(lax.div(v, b), 2)
    return v


def dot(a, b):
    return lax.dot_general(a, b, (((1,), (0,)), ((), ())), preferred_element_type=f32)


def dot_nt(a, b):
    return lax.dot_general(a, b, (((1,), (1,)), ((), ())), preferred_element_type=f32)


def dot_tn(a, b):
    return lax.dot_general(a, b, (((0,), (0,)), ((), ())), preferred_element_type=f32)


def inv_rms(v):
    return lax.rsqrt(jnp.mean(v * v, axis=-1, keepdims=True) + epsilon)


def norm_back(v, gain, w):
    r = inv_rms(v)
    gw = gain * w
    mean = jnp.mean(gw * v, axis=-1, keepdims=True)
    return r * gw - v * (r * r * r * mean), jnp.sum(w * (v * r), axis=0, keepdims=True)


def gelu_parts(gate):
    sq = gate * gate
    th = jnp.tanh(GELU_A * gate * (1.0 + GELU_B * sq))
    half = 0.5 * (1.0 + th)
    slope = half + 0.5 * gate * (1.0 - th * th) * (GELU_A * (1.0 + 3.0 * GELU_B * sq))
    return gate * half, slope


def softmax(scores):
    e = jnp.exp(scores - jnp.max(scores, axis=-1, keepdims=True))
    return (e * (1.0 / jnp.sum(e, axis=-1, keepdims=True))).astype(bf16)


def pad64(v):
    return jnp.concatenate([v, jnp.zeros((v.shape[0], 64), v.dtype)], axis=1)


def above64(v):
    return jnp.concatenate([jnp.zeros((v.shape[0], 64), v.dtype), v], axis=1)


def pack(ref, slot, parts):
    ref[slot, 0:256, :] = jnp.concatenate([parts[0], parts[1]], axis=1)
    ref[slot, 256:384, :] = jnp.concatenate([parts[2][0:128], parts[2][128:256]], axis=1)


def unpack(ref, slot):
    two = ref[slot, 0:256, :]
    last = ref[slot, 256:384, :]
    return (two[:, :64], two[:, 64:], jnp.concatenate([last[:, :64], last[:, 64:]], axis=0))


def assemble(ref, dst):
    for t in range(2):
        a = unpack(ref, 2 * t) + unpack(ref, 2 * t + 1)
        for j in range(3):
            at = 384 * t + 128 * j
            dst[:, at : at + 128] = jnp.concatenate([a[2 * j], a[2 * j + 1]], axis=1)


def disperse(val, ref):
    for gg in range(4):
        pack(ref, gg, [val[:, 192 * gg + 64 * h : 192 * gg + 64 * h + 64] for h in range(3)])


def block(i):
    return pl.ds(pl.multiple_of(i * 256, 256), 256)


def layer_kernel(
    x, mem, cot, segs, gain1, gain2, gain3, rel, buck, live, w_in, w_kv, w_ao, w_cq, w_co, w_gu, w_dn,
    out, gin, gmem, o_gu, o_dn, o_b, o_q, o_m, o_small,
    *,
    xrow, mrow, h1, wQ, wM, W3, wgu, wd, sm, sg, gains, lines, hot, tbias, qh, kh, vh, mkv, p_self, p_cross,
    opack, arecv, attn, qpack, qrecv, crecv, cattn, after_self, after_cross, h2, h3, prod, dgu, cotb, frecv,
    hrecv, outb, grad, low, dcq, acc, dqkv, rs1, rs2, rt1, rt2, gur, dnr, bsib, bdp, qdp, mdp, zg1, zg2, zd1, zd2,
    zb1, zb2, qfar, mfar, gsm, sm1, sm2, sgown, ssem, rsem, lsem,
):
    drecv, dqrecv, srecv = arecv, crecv, qrecv
    fown, fpart, xown = tbias.at[2], outb, after_cross
    keep, hpart = p_cross.at[0], low.at[1]

    d, s = lax.axis_index("dp"), lax.axis_index("seq")
    c, z, g, r = lax.rem(s, 2), lax.div(s, 2), lax.rem(s, 4), lax.div(s, 4)
    used = {"remote": 0, "local": 0}
    flying = []

    def remote(src, dst, send_sem, recv_sem, dev):
        return pltpu.make_async_remote_copy(
            src_ref=src, dst_ref=dst, send_sem=ssem.at[send_sem], recv_sem=rsem.at[recv_sem],
            device_id=dev, device_id_type=MESH,
        )

    def fresh(n=1):
        used["remote"] += n
        assert used["remote"] <= N_SEM
        return used["remote"] - n

    def push(src, dst, dev):
        sem = fresh()
        copy = remote(src, dst, sem, sem, dev)
        copy.start()
        flying.append(copy)
        return copy

    def sent(copies):
        for copy in copies:
            copy.wait_send()
            flying[:] = [other for other in flying if other is not copy]

    def arrived(copies):
        for copy in copies:
            copy.wait_recv()

    def local(src, dst):
        copy = pltpu.make_async_copy(src, dst, lsem.at[used["local"]])
        used["local"] += 1
        copy.start()
        return copy

    def dpk(k):
        return (flip(d, k, 2), s)

    def seqk(k):
        return (d, flip(s, k, 3))

    class Gather:
        def __init__(self, whole, part):
            self.part = part
            own = whole(d)
            self.first = {k: push(own, own, dpk(k)) for k in (1, 2)}
            self.second = []

        def relay(self):
            for k, half in ((1, 0), (2, 1)):
                arrived([self.first[k]])
                src = self.part(flip(d, k, 2), half)
                self.second.append(push(src, src, dpk(3 - k)))

        def done(self):
            arrived(self.second)

        def gone(self):
            sent([*self.first.values(), *self.second])

    class Reduce:
        def __init__(self, part, got):
            self.part, self.got = part, got
            self.first = {}
            for k, half in ((1, 0), (2, 1)):
                for j, kk in ((0, k), (1, 3)):
                    copy = push(part(flip(d, kk, 2), half), got.at[3 * half + j], dpk(k))
                    self.first[half, j] = copy

        def middle(self):
            self.second = {}
            for k, half in ((1, 0), (2, 1)):
                arrived([self.first[half, 1]])
                ref = self.part(flip(d, 3 - k, 2), half)
                ref[...] = (ref[...].astype(f32) + self.got[3 * half + 1].astype(f32)).astype(bf16)
                self.second[half] = push(ref, self.got.at[3 * half + 2], dpk(3 - k))

        def end(self):
            for half in (0, 1):
                arrived([self.first[half, 0], self.second[half]])
                ref = self.part(d, half)
                total = ref[...].astype(f32) + self.got[3 * half].astype(f32) + self.got[3 * half + 2].astype(f32)
                ref[...] = total.astype(bf16)

    def moved(srcs, dsts, devs, slot):
        base = fresh(2)
        for i in range(2):
            away = remote(srcs[i], dsts[i], base + i, base + slot, (d, devs[i]))
            here = pltpu.make_async_copy(srcs[i], dsts[i], rsem.at[base + slot])

            @pl.when(devs[i] != s)
            def _():
                away.start()

            @pl.when(devs[i] == s)
            def _():
                here.start()

        def wait_recv(places):
            for i in range(2):
                pltpu.make_async_copy(places[i], places[i], rsem.at[base + i]).wait()

        def wait_send():
            for i in range(2):
                away = remote(srcs[i], dsts[i], base + i, base + slot, (d, devs[i]))

                @pl.when(devs[i] != s)
                def _():
                    away.wait_send()

        return wait_recv, wait_send

    mine, mine_d = pl.ds(pl.multiple_of(d * 192, 64), 192), block(d)
    here = pl.ds(s * 128, 128)
    own_x = local(x.at[r], xrow.at[here])
    stage = [p_self.at[0, i, 0:192] for i in range(4)] + [p_self.at[1, 0, 0:192]]
    own_in = [
        local(w.at[:, 768 * i : 768 * i + 768], stage[p])
        for p, (w, i) in enumerate(((w_in, 0), (w_in, 1), (w_in, 2), (w_kv, 0), (w_kv, 1)))
    ]
    own_W3 = [local(w, W3.at[i, mine]) for i, w in enumerate((w_ao, w_cq, w_co))]
    own_m = local(mem.at[r], mrow.at[here])
    own_gu = []
    for p in range(8):
        at = pl.multiple_of((p // 4) * FF + (p % 4) * 512 + c * 256, 256)
        own_gu.append(local(w_gu.at[:, pl.ds(at, 256)], wgu.at[mine, pl.ds(512 * (p % 4) + 256 * (p // 4), 256)]))
    own_dn = local(w_dn.at[block(c)], wd.at[mine_d])

    barrier = pltpu.get_barrier_semaphore()
    peers = [dpk(k) for k in (1, 2, 3)] + [seqk(k) for k in range(1, 8)]
    for p in peers:
        pl.semaphore_signal(barrier, inc=1, device_id=p, device_id_type=MESH)
    for i in range(2):
        sgown[i] = jnp.broadcast_to(segs[i : i + 1, :].astype(f32), (16, 128)).astype(bf16)
    sg[s] = sgown[r]
    at_bucket = lax.broadcasted_iota(jnp.int32, (8, 128), 1) == lax.broadcasted_iota(jnp.int32, (8, 128), 0) + 8 * d
    gains[...] = jnp.zeros((16, 768), f32)
    gains[0:12, 0:128] = dot_tn(rel[...].astype(f32), at_bucket.astype(f32))
    for q in range(4):

        @pl.when(d == q)
        def _():
            for i, gain in enumerate((gain1, gain2, gain3)):
                gains[12 + i : 13 + i, 192 * q : 192 * q + 192] = gain[...].astype(f32).reshape(1, 192)

    sm[d] = gains[...].astype(bf16)
    pl.semaphore_wait(barrier, len(peers))

    def row_of(k):
        return lax.div(flip(s, k, 3), 4)

    def spread(src, dst):
        return {m: push(src.at[row_of(2 * m)], dst.at[here], seqk(2 * m)) for m in (1, 2, 3)}

    def hand_on(dst, m):
        part = dst.at[pl.ds(flip(s, 2 * m, 3) * 128, 128)]
        return push(part, part, seqk(1))

    sm_in = [push(sm.at[d], sm.at[d], dpk(k)) for k in (1, 2, 3)]
    sg_in = [push(sgown.at[row_of(k)], sg.at[s], seqk(k)) for k in range(1, 8)]
    xd = spread(x, xrow)
    own_x.wait()
    xs = {0: hand_on(xrow, 0)}
    for cp in own_in:
        cp.wait()
    for q in range(4):

        @pl.when(g == q)
        def _():
            for p in range(5):
                dst, at = (wQ, 192 * p) if p < 3 else (wM, 192 * (p - 3))
                dst[mine, at : at + 192] = stage[p][:, 192 * q : 192 * q + 192]

    def part192(ref):
        return lambda dd, half: ref.at[pl.ds(pl.multiple_of(dd * 192 + 96 * half, 32), 96)]

    def whole192(ref):
        return lambda dd: ref.at[pl.ds(pl.multiple_of(dd * 192, 64), 192)]

    def part_dn(dd, half):
        return wd.at[pl.ds(pl.multiple_of(dd * 256 + 128 * half, 128), 128)]

    def part_b(i):
        return lambda dd, half: W3.at[i, pl.ds(pl.multiple_of(dd * 192 + c * 96 + 48 * half, 16), 48)]

    q_w = Gather(whole192(wQ), part192(wQ))

    def half_rows(dd, cc):
        return pl.ds(pl.multiple_of(dd * 192 + cc * 96, 32), 96)

    def send_W3(i):
        own_W3[i].wait()
        return Gather(lambda dd: W3.at[i, half_rows(dd, c)], part_b(i))

    def share_W3(i):
        W3_w[i].done()
        return [push(W3.at[i, rows], W3.at[i, rows], seqk(1)) for rows in (half_rows(flip(d, k, 2), c) for k in (1, 2, 3))]

    m_w = Gather(whole192(wM), part192(wM))
    W3_w = {0: send_W3(0)}
    W3_sib = {}

    arrived(sm_in)
    total = sm[0].astype(f32)
    for i in range(1, 4):
        total += sm[i].astype(f32)
    gains[...] = total
    near = jnp.concatenate([buck[i : i + 1, :] for i in range(4)], axis=1)
    by_dist = (lax.broadcasted_iota(jnp.int32, (128, 512), 0) == near).astype(bf16)
    turn = lax.broadcasted_iota(jnp.int32, (512, 1024), 0) + lax.broadcasted_iota(jnp.int32, (512, 1024), 1) == 768
    hot[...] = dot(by_dist, turn.astype(bf16)).astype(bf16)
    column = lax.broadcasted_iota(jnp.int32, (16, 1024), 1)
    line = dot(total[:, :128].astype(bf16), hot[...])
    lines[...] = jnp.where((column > 256) & (column < 769), line, masked_score)
    for h in range(3):
        row = jnp.broadcast_to(lines[pl.ds(3 * g + h, 1), :], (256, 1024))
        tbias[h] = pltpu.roll(row, 0, 1, stride=1, stride_axis=0)[:, 256:]

    def norm_block(m):
        rows = block(flip(z, m, 2))
        val = xrow[rows, :].astype(f32)
        h1[rows, :] = (val * inv_rms(val) * gains[12:13, :]).astype(bf16)

    arrived([xs[0]])
    norm_block(0)
    for m in (1, 2):
        arrived([xd[m]])
        xs[m] = hand_on(xrow, m)
    q_w.relay()
    arrived([xs[1]])
    norm_block(1)
    m_w.relay()
    W3_w[1] = send_W3(1)
    arrived([xd[3]])
    xs[3] = hand_on(xrow, 3)
    md = spread(mem, mrow)
    own_m.wait()
    ms = {0: hand_on(mrow, 0)}
    W3_w[0].relay()
    W3_w[2] = send_W3(2)
    arrived([xs[2]])
    norm_block(2)
    arrived([xs[3]])
    norm_block(3)

    arrived(sg_in)
    lane64 = lax.broadcasted_iota(jnp.int32, (128, 64), 1).astype(f32)
    inside = lane64 < 3.5
    for h in range(3):
        beyond = lax.broadcasted_iota(jnp.int32, (512, 128), 1) >= 64
        kh[h, 0:512, :] = jnp.where(beyond, -1.0, 0.0).astype(bf16)
        vh[h, 0:512, :] = jnp.zeros((512, 128), bf16)
    q_w.done()

    def project(i, carry):
        rows = block(i)
        res = dot(h1[rows, :], wQ[...]).astype(bf16)
        qa, ka = [], []
        for j in range(2):
            seg = sg[2 * i + j, 0:1, :].astype(f32)
            same = jnp.transpose(jnp.broadcast_to(seg, (128, 128)))[:, :64] == lane64
            qa.append(jnp.where(same, BIG, 0.0))
            ka.append(jnp.where(inside & jnp.logical_not(same), -1.0, 0.0))
        qa = jnp.concatenate(qa, axis=0).astype(bf16)
        ka = jnp.concatenate(ka, axis=0).astype(bf16)
        lower = pl.ds(pl.multiple_of(i * 256 + 512, 256), 256)
        for h in range(3):
            qv = (res[:, 64 * h : 64 * h + 64].astype(f32) * SCALE).astype(bf16)
            qh[h, rows, :] = jnp.concatenate([qv, qa], axis=1)
            kh[h, lower, :] = jnp.concatenate([res[:, 192 + 64 * h : 256 + 64 * h], ka], axis=1)
            vh[h, lower, :] = pad64(res[:, 384 + 64 * h : 448 + 64 * h])
        return carry

    lax.fori_loop(0, 4, project, 0)

    for cp in own_gu:
        cp.wait()
    gu_w = Gather(whole192(wgu), part192(wgu))
    W3_w[1].relay()

    def window(b):
        return pl.ds(pl.multiple_of(b * 256, 256), 768)

    a_in = []
    for k in (2, 3, 1, 0):
        b = flip(g, k, 2)
        parts = []
        for h in range(3):
            p = softmax(dot_nt(qh[h, block(b), :], kh[h, window(b), :]) + tbias[h])
            p_self[h, b] = p
            parts.append(dot(p, vh[h, window(b), :])[:, :64].astype(bf16))
        if k == 0:
            pack(arecv, g, parts)
        else:
            pack(opack, b, parts)
            a_in.append(push(opack.at[b], arecv.at[g], seqk(k)))
        if k == 2:
            W3_w[2].relay()

    own_dn.wait()
    dn_w = Gather(lambda dd: wd.at[block(dd)], part_dn)
    for m in (1, 2, 3):
        arrived([md[m]])
        ms[m] = hand_on(mrow, m)
    halves = [cotb.at[c, pl.ds(c * 128, 128)]] * 2
    dests = [4 * rr + z for rr in range(2)]
    cslot = lax.rem(z, 2)
    cot_recv, cot_sent = moved(
        [cot.at[0], cot.at[1]], [cotb.at[cslot, pl.ds(c * 128, 128)]] * 2, dests, c
    )
    W3_sib[0] = share_W3(0)
    m_w.done()
    arrived(ms.values())

    def project_memory(i, carry):
        rows = block(i)
        res = dot(mrow[rows, :], wM[...]).astype(bf16)
        for h in range(3):
            mkv[h, rows, :] = jnp.concatenate(
                [res[:, 64 * h : 64 * h + 64], res[:, 192 + 64 * h : 256 + 64 * h]], axis=1
            )
        return carry

    lax.fori_loop(0, 4, project_memory, 0)
    W3_sib[1] = share_W3(1)

    arrived(a_in)
    assemble(arecv, attn)
    arrived(W3_sib[0])
    alive = live[r].astype(f32)
    res = xrow[block(g), :].astype(f32) + alive * dot(attn[...], W3[0])
    after_self[...] = res
    h2[...] = (res * inv_rms(res) * gains[13:14, :]).astype(bf16)
    arrived(W3_sib[1])
    disperse((dot(h2[...], W3[1]).astype(bf16).astype(f32) * SCALE).astype(bf16), qpack)
    q_in = {k: push(qpack.at[flip(g, k, 2)], qrecv.at[g], seqk(k)) for k in (2, 3, 1)}
    qrecv[g] = qpack[g]
    gu_w.relay()
    cot_recv([cotb.at[c, pl.ds(0, 128)], cotb.at[c, pl.ds(128, 128)]])
    cot_sib = push(cotb.at[c], cotb.at[c], seqk(1))

    sent(a_in)
    c_in = []
    for k in (0, 1, 2, 3):
        b = flip(g, k, 2)
        if k:
            arrived([q_in[k]])
        qs = unpack(qrecv, b)
        parts = []
        for h in range(3):
            p = softmax(dot_nt(pad64(qs[h]), mkv[h]))
            p_cross[h, b] = p
            parts.append(dot(p, mkv[h])[:, 64:].astype(bf16))
        if k == 0:
            pack(crecv, g, parts)
        else:
            pack(opack, b, parts)
            c_in.append(push(opack.at[b], crecv.at[g], seqk(k)))
        if k == 0:
            W3_sib[2] = share_W3(2)
        if k == 1:
            dn_w.relay()
    arrived(W3_sib[2])
    arrived(c_in)
    assemble(crecv, cattn)
    res = after_self[...] + alive * dot(cattn[...], W3[2])
    after_cross[...] = res
    h3[c] = (res * inv_rms(res) * gains[14:15, :]).astype(bf16)
    h3_in = push(h3.at[c], h3.at[c], seqk(1))
    arrived([cot_sib])
    gu_w.done()
    dn_w.done()
    arrived([h3_in])

    gu_w.gone()
    dn_w.gone()
    tbias[0:2] = jnp.zeros((2, 256, 768), f32)

    def feed_forward(n, carry):
        cols = block(n)
        both = pl.ds(pl.multiple_of(n * 512, 512), 512)
        gates, ups = pl.ds(pl.multiple_of(n * 512, 512), 256), pl.ds(pl.multiple_of(n * 512 + 256, 256), 256)
        for t in range(2):
            gate, up = dot(h3[t], wgu[:, gates]), dot(h3[t], wgu[:, ups])
            act, slope = gelu_parts(gate)
            prod[t, :, cols] = (act * up).astype(bf16)
            gp = dot_nt((cotb[t].astype(f32) * alive).astype(bf16), wd[cols, :])
            dgu[t, :, gates] = (gp * up * slope).astype(bf16)
            dgu[t, :, ups] = (gp * act).astype(bf16)
            tbias[t] += dot_nt(dgu[t, :, both], wgu[:, both])
        for part in (gates, ups):
            wgu[:, part] = dot_tn(h3[...].reshape(512, 768), dgu[:, :, part].reshape(512, 256)).astype(bf16)
        return carry

    def grad_dn(n, carry):
        cols = block(n)
        down_in = (cotb[...].astype(f32) * alive).astype(bf16).reshape(512, 768)
        wd[cols, :] = dot_tn(prod[:, :, cols].reshape(512, 256), down_in).astype(bf16)
        return carry

    def part_gu(i):
        cols = pl.ds(1024 * i, 1024)
        return lambda dd, half: wgu.at[pl.ds(pl.multiple_of(dd * 192 + 96 * half, 32), 96), cols]

    far_side = lax.div(z, 2)
    outer = lax.rem(z, 2) == far_side
    inner = jnp.logical_not(outer)

    def push_if(src, dst, dev, sends, gets):
        copy = remote(src, dst, fresh(1), used["remote"] - 1, dev)

        class Copy:
            def wait_send(self):
                pl.when(sends)(copy.wait_send)

            def wait_recv(self):
                pl.when(gets)(copy.wait_recv)

        pl.when(sends)(copy.start)
        res = Copy()
        flying.append(res)
        return res

    class Around:
        def __init__(self, own, out, half, got):
            self.own, self.out, self.half, self.got = own, out, half, got

        def add(self, ref, got):
            @pl.when(inner)
            def _():
                ref[...] = (ref[...].astype(f32) + got[...].astype(f32)).astype(bf16)

        def step1(self):
            self.copy = push_if(self.own, self.got[0], seqk(2), outer, inner)

        def step2(self):
            arrived([self.copy])
            self.add(self.own, self.got[0])
            self.copy = push_if(self.half(self.own, 1 - far_side), self.got[1], seqk(6), inner, inner)

        def step3(self):
            arrived([self.copy])
            src, dst = self.half(self.own, far_side), self.half(self.out, far_side)
            self.add(src, self.got[1])
            self.copy = push_if(src, dst, seqk(6), inner, inner)
            self.back = [push_if(src, dst, seqk(2), inner, outer)]
            self.keep = pltpu.make_async_copy(src, dst, lsem.at[used["local"]])
            used["local"] += 1
            pl.when(inner)(self.keep.start)

        def step4(self):
            arrived([self.copy])
            pl.when(inner)(self.keep.wait)
            place = self.half(self.out, 1 - far_side)
            self.back.append(push_if(place, place, seqk(2), inner, outer))

        def step5(self):
            arrived(self.back)
            self.copy = push(self.out, self.out, seqk(1))

    def halves(n):
        return lambda ref, i: ref.at[pl.ds(pl.multiple_of(n * i, 16), n)]

    cols_gu = [pl.ds(1024 * i, 1024) for i in range(2)]
    g_z, u_z = [
        Around(wgu.at[mine, cols_gu[i]], o_gu.at[c, :, cols_gu[i]], halves(96), (zg1.at[i], zg2.at[i])) for i in range(2)
    ]
    n_z = Around(wd.at[mine_d], o_dn.at[c], halves(128), (zd1, zd2))
    b_z = [Around(W3.at[i, half_rows(d, c)], o_b.at[i, c], halves(48), (zb1.at[i], zb2.at[i])) for i in range(3)]

    lax.fori_loop(0, 2, feed_forward, 0)
    g_rs = Reduce(part_gu(0), gur.at[0])
    lax.fori_loop(2, 4, feed_forward, 0)
    u_rs = Reduce(part_gu(1), gur.at[1])
    hpart[...] = tbias[1 - c].astype(bf16)
    h_in = push(hpart, hrecv, seqk(1))
    fpart[...] = dot(prod[1 - c], wd[...]).astype(bf16)
    f_in = push(fpart, frecv, seqk(1))
    arrived([h_in])
    dv, dgain3 = norm_back(after_cross[...], gains[14:15, :], tbias[c] + hrecv[...].astype(f32))
    gsm[...] = jnp.zeros((16, 768), f32)
    gsm[14:15, :] = dgain3
    grad[...] = cotb[c].astype(f32) + dv
    low[0] = (grad[...] * alive).astype(bf16)
    sent(c_in)
    sent(q_in.values())
    disperse(dot_nt(low[0], W3[2]).astype(bf16), opack)
    d_in = {k: push(opack.at[flip(g, k, 2)], drecv.at[g], seqk(k)) for k in (2, 3, 1)}
    drecv[g] = opack[g]
    g_rs.middle()
    fown[...] = dot(prod[c], wd[...])
    lax.fori_loop(0, 4, grad_dn, 0)

    arrived([f_in])
    sent([f_in])
    outb[...] = (after_cross[...] + alive * (fown[...] + frecv[...].astype(f32))).astype(bf16)
    back = [2 * g + j for j in range(2)]
    out_recv, out_sent = moved([outb.at[pl.ds(0, 128)], outb.at[pl.ds(128, 128)]], [out.at[r]] * 2, back, r)

    lefts = (attn, h2, cattn)
    rights = (low.at[1], dcq, low.at[0])
    b_sib = {}

    def grad_square(i):
        W3_w[i].gone()
        sent(W3_sib[i])
        W3[i] = dot_tn(lefts[i][...], rights[i][...]).astype(bf16)
        b_sib[i] = [push(W3.at[i, half_rows(q, 1 - c)], bsib.at[i, q], seqk(1)) for q in range(4)]

    def chip_square(i):
        arrived(b_sib[i])
        for q in range(4):
            rows = half_rows(q, c)
            W3[i, rows, :] = (W3[i, rows, :].astype(f32) + bsib[i, q].astype(f32)).astype(bf16)
        return Reduce(part_b(i), bdp.at[i])

    grad_square(2)

    for h in range(3):
        acc[h, 0:1024, :] = jnp.zeros((1024, 128), f32)
    dq_in = []

    def cross_back(k):
        b = flip(g, k, 2)
        if k:
            arrived([d_in[k]])
        dos, qs = unpack(drecv, b), unpack(qrecv, b)
        parts = []
        for h in range(3):
            p = p_cross[h, b]
            do = above64(dos[h])
            dp = dot_nt(do, mkv[h])
            pf = p.astype(f32)
            ds = (pf * (dp - jnp.sum(dp * pf, axis=-1, keepdims=True))).astype(bf16)
            parts.append((dot(ds, mkv[h])[:, :64] * SCALE).astype(bf16))
            acc[h, 0:1024, :] += dot_tn(ds, pad64(qs[h])) + dot_tn(p, do)
        if k == 0:
            pack(dqrecv, g, parts)
        else:
            pack(qpack, b, parts)
            dq_in.append(push(qpack.at[b], dqrecv.at[g], seqk(k)))

    cross_back(2)
    n_rs = Reduce(part_dn, dnr)
    cross_back(3)
    u_rs.middle()
    cross_back(1)
    g_rs.end()
    g_z.step1()
    cross_back(0)
    b_rs = {2: chip_square(2)}

    def keep_memory(i, carry):
        rows = block(i)
        vals = [acc[h, rows, :][:, :64] for h in range(3)] + [acc[h, rows, :][:, 64:] for h in range(3)]
        dqkv[rows, 0:384] = jnp.concatenate(vals, axis=1).astype(bf16)
        return carry

    lax.fori_loop(0, 4, keep_memory, 0)
    arrived(dq_in)
    assemble(dqrecv, dcq)
    dv, dgain2 = norm_back(after_self[...], gains[13:14, :], dot_nt(dcq[...], W3[1]))
    gsm[13:14, :] = dgain2
    grad[...] += dv
    sent([h_in])
    low[1] = (grad[...] * alive).astype(bf16)
    sent(d_in.values())
    disperse(dot_nt(low[1], W3[0]).astype(bf16), opack)
    s_in = {k: push(opack.at[flip(g, k, 2)], srecv.at[g], seqk(k)) for k in (2, 3, 1)}
    srecv[g] = opack[g]

    u_rs.end()
    u_z.step1()
    n_rs.middle()
    grad_square(1)
    grad_square(0)

    class Rows:
        def __init__(self, compute, first, second):
            self.compute, self.first, self.second = compute, first, second
            self.in3 = push(compute(flip(g, 3, 2)), first.at[0], seqk(1))
            self.part2 = compute(flip(g, 2, 2))
            self.in1 = push(compute(flip(g, 1, 2)), first.at[1], seqk(1))

        def far(self):
            arrived([self.in3])
            self.part2[...] = (self.part2[...].astype(f32) + self.first[0].astype(f32)).astype(bf16)
            self.out = push(self.part2, self.second, seqk(2))
            self.part0 = self.compute(g)

        def total(self):
            arrived([self.in1, self.out])
            return self.part0[...].astype(f32) + self.first[1].astype(f32) + self.second[...].astype(f32)

    m_w.gone()
    sent(ms.values())
    for i in range(3):
        keep[i, :, 0:384] = dot_tn(mrow[:, 256 * i : 256 * i + 256], dqkv[:, 0:384]).astype(bf16)

    def memory_part(b):
        mrow[block(b), :] = dot_nt(dqkv[block(b), 0:384], wM[...]).astype(bf16)
        return mrow.at[block(b)]

    m_rows = Rows(memory_part, rt1, rt2)
    m_rows.far()
    for i in range(3):
        wM[256 * i : 256 * i + 256, :] = keep[i, :, 0:384]

    g_z.step2()
    m_rs = Reduce(part192(wM), mdp)

    for h in range(3):
        acc[h] = jnp.zeros((1536, 128), f32)
        tbias[h] = jnp.zeros((256, 768), f32)

    def self_back(k):
        b = flip(g, k, 2)
        if k:
            arrived([s_in[k]])
        dos = unpack(srecv, b)
        for h in range(3):
            p = p_self[h, b]
            do = pad64(dos[h])
            dp = dot_nt(do, vh[h, window(b), :])
            pf = p.astype(f32)
            ds = pf * (dp - jnp.sum(dp * pf, axis=-1, keepdims=True))
            tbias[h] += ds
            ds = ds.astype(bf16)
            dqkv[block(b), 64 * h : 64 * h + 64] = (dot(ds, kh[h, window(b), :])[:, :64] * SCALE).astype(bf16)
            acc[h, window(b), :] += dot_tn(ds, pad64(qh[h, block(b), :][:, :64])) + dot_tn(p, above64(dos[h]))

    self_back(0)
    b_rs[1] = chip_square(1)
    b_rs[0] = chip_square(0)
    n_rs.end()
    n_z.step1()
    g_z.step3()
    self_back(2)
    m_rs.middle()
    b_rs[2].middle()
    u_z.step2()
    self_back(3)
    g_z.step4()

    total = m_rows.total()
    out_recv([out.at[0], out.at[1]])
    out_sent()
    outb[...] = total.astype(bf16)
    mem_recv, mem_sent = moved([outb.at[pl.ds(0, 128)], outb.at[pl.ds(128, 128)]], [gmem.at[r]] * 2, back, r)

    self_back(1)
    u_z.step3()

    def keep_self(i, carry):
        rows, lower = block(i), pl.ds(pl.multiple_of(i * 256 + 512, 256), 256)
        for h in range(3):
            dqkv[rows, 192 + 64 * h : 256 + 64 * h] = acc[h, lower, :][:, :64].astype(bf16)
            dqkv[rows, 384 + 64 * h : 448 + 64 * h] = acc[h, lower, :][:, 64:].astype(bf16)
        return carry

    lax.fori_loop(0, 4, keep_self, 0)
    xown[...] = xrow[block(g), :].astype(f32)
    sent(xs.values())

    def self_part(b):
        xrow[block(b), :] = dot_nt(dqkv[block(b), :], wQ[...]).astype(bf16)
        return xrow.at[block(b)]

    x_rows = Rows(self_part, rs1, rs2)
    x_rows.far()
    m_rs.end()
    m_far = push(wM.at[mine], mfar, seqk(4))
    b_rs[1].middle()
    b_rs[0].middle()
    n_z.step2()
    q_w.gone()

    def grad_qkv(n, carry):
        cols = pl.ds(pl.multiple_of(n * 128, 128), 128)
        wQ[cols, :] = dot_tn(h1[:, cols], dqkv[...]).astype(bf16)
        return carry

    lax.fori_loop(0, 6, grad_qkv, 0)
    q_rs = Reduce(part192(wQ), qdp)

    b_rs[2].end()
    b_z[2].step1()

    for h in range(3):
        wide = jnp.concatenate([jnp.zeros((256, 256), f32), tbias[h]], axis=1)
        rows = lax.broadcasted_iota(jnp.int32, (256, 1024), 0)
        for i in range(8):
            bit = lax.rem(lax.div(rows, 1 << i), 2) == 1
            wide = jnp.where(bit, pltpu.roll(wide, 1024 - (1 << i), 1), wide)
        lines[h : h + 1, :] = jnp.sum(wide, axis=0, keepdims=True)
    val = lines[...]
    top = val.astype(bf16)
    rest = val - top.astype(f32)
    mid = rest.astype(bf16)
    last = (rest - mid.astype(f32)).astype(bf16)
    by_bucket = dot_nt(top, hot[...]) + dot_nt(mid, hot[...]) + dot_nt(last, hot[...])
    row16 = lax.broadcasted_iota(jnp.int32, (16, 128), 0)
    spot = jnp.zeros((16, 128), f32)
    for h in range(3):
        spot = jnp.where(row16 == 3 * g + h, jnp.broadcast_to(by_bucket[h : h + 1, :], (16, 128)), spot)
    gsm[:, 0:128] += spot

    for i in (1, 0):
        b_rs[i].end()
        b_z[i].step1()
    u_z.step4()
    g_z.step5()
    n_z.step3()
    q_rs.middle()

    b_z[2].step2()
    q_rs.end()
    q_far = push(wQ.at[mine], qfar, seqk(4))

    dv, dgain1 = norm_back(xown[...], gains[12:13, :], x_rows.total())
    gsm[12:13, :] = dgain1
    sm_dp = [push(gsm, sm1.at[k - 1], dpk(k)) for k in (1, 2, 3)]
    mem_recv([gmem.at[0], gmem.at[1]])
    mem_sent()
    outb[...] = (grad[...] + dv).astype(bf16)
    gin_recv, gin_sent = moved([outb.at[pl.ds(0, 128)], outb.at[pl.ds(128, 128)]], [gin.at[r]] * 2, back, r)

    def far_sum(ref, copy, got, place):
        arrived([copy])
        sent([copy])
        ref[mine, :] = (ref[mine, :].astype(f32) + got[...].astype(f32)).astype(bf16)
        here_too = local(ref.at[mine], place.at[g])
        return here_too, push(ref.at[mine], place.at[g], seqk(2)), push(ref.at[mine], place.at[g], seqk(1))

    m_own, m_pair, m_s1 = far_sum(wM, m_far, mfar, o_m)
    n_z.step4()
    u_z.step5()
    b_z[1].step2()
    b_z[0].step2()
    b_z[2].step3()
    arrived(sm_dp)
    sent(sm_dp)
    gsm[...] = gsm[...] + sm1[0] + sm1[1] + sm1[2]
    sm_seq = [push(gsm, sm2.at[k - 1], seqk(k)) for k in range(1, 8)]
    q_own, q_pair, q_s1 = far_sum(wQ, q_far, qfar, o_q)
    b_z[1].step3()
    b_z[0].step3()
    b_z[2].step4()
    n_z.step5()
    b_z[1].step4()
    b_z[0].step4()
    arrived(sm_seq)
    val = gsm[...]
    for k in range(7):
        val = val + sm2[k]
    o_small[...] = val
    other = flip(g, 2, 2)
    arrived([m_pair])
    m_s2 = push(o_m.at[other], o_m.at[other], seqk(1))
    arrived([q_pair])
    q_s2 = push(o_q.at[other], o_q.at[other], seqk(1))
    for i in (2, 1, 0):
        b_z[i].step5()
    gin_recv([gin.at[0], gin.at[1]])
    gin_sent()
    cot_sent()
    m_own.wait()
    q_own.wait()
    arrived([m_s1, q_s1, m_s2, q_s2])
    for chain in (g_z, u_z, n_z, *b_z):
        arrived([chain.copy])
    for cp in list(flying):
        cp.wait_send()


def scratch():
    def vm(kind, *shape):
        return pltpu.VMEM(shape, kind)

    return dict(
        xrow=vm(bf16, 1024, 768),
        mrow=vm(bf16, 1024, 768),
        h1=vm(bf16, 1024, 768),
        wQ=vm(bf16, 768, 576),
        wM=vm(bf16, 768, 384),
        W3=vm(bf16, 3, 768, 768),
        wgu=vm(bf16, 768, 2048),
        wd=vm(bf16, 1024, 768),
        sm=vm(bf16, 4, 16, 768),
        sg=vm(bf16, 8, 16, 128),
        gains=vm(f32, 16, 768),
        lines=vm(f32, 16, 1024),
        hot=vm(bf16, 128, 1024),
        tbias=vm(f32, 3, 256, 768),
        qh=vm(bf16, 3, 1024, 128),
        kh=vm(bf16, 3, 1536, 128),
        vh=vm(bf16, 3, 1536, 128),
        mkv=vm(bf16, 3, 1024, 128),
        p_self=vm(bf16, 3, 4, 256, 768),
        p_cross=vm(bf16, 3, 4, 256, 1024),
        opack=vm(bf16, 4, 384, 128),
        arecv=vm(bf16, 4, 384, 128),
        attn=vm(bf16, 256, 768),
        qpack=vm(bf16, 4, 384, 128),
        qrecv=vm(bf16, 4, 384, 128),
        crecv=vm(bf16, 4, 384, 128),
        cattn=vm(bf16, 256, 768),
        after_self=vm(f32, 256, 768),
        after_cross=vm(f32, 256, 768),
        h2=vm(bf16, 256, 768),
        h3=vm(bf16, 2, 256, 768),
        prod=vm(bf16, 2, 256, 1024),
        dgu=vm(bf16, 2, 256, 2048),
        cotb=vm(bf16, 2, 256, 768),
        frecv=vm(bf16, 256, 768),
        hrecv=vm(bf16, 256, 768),
        outb=vm(bf16, 256, 768),
        grad=vm(f32, 256, 768),
        low=vm(bf16, 2, 256, 768),
        dcq=vm(bf16, 256, 768),
        acc=vm(f32, 3, 1536, 128),
        dqkv=vm(bf16, 1024, 576),
        rs1=vm(bf16, 2, 256, 768),
        rs2=vm(bf16, 256, 768),
        rt1=vm(bf16, 2, 256, 768),
        rt2=vm(bf16, 256, 768),
        gur=vm(bf16, 2, 6, 96, 1024),
        dnr=vm(bf16, 6, 128, 768),
        bsib=vm(bf16, 3, 4, 96, 768),
        bdp=vm(bf16, 3, 6, 48, 768),
        qdp=vm(bf16, 6, 96, 576),
        mdp=vm(bf16, 6, 96, 384),
        zg1=vm(bf16, 2, 192, 1024),
        zg2=vm(bf16, 2, 96, 1024),
        zd1=vm(bf16, 256, 768),
        zd2=vm(bf16, 128, 768),
        zb1=vm(bf16, 3, 96, 768),
        zb2=vm(bf16, 3, 48, 768),
        qfar=vm(bf16, 192, 576),
        mfar=vm(bf16, 192, 384),
        gsm=vm(f32, 16, 768),
        sm1=vm(f32, 3, 16, 768),
        sm2=vm(f32, 7, 16, 768),
        sgown=vm(bf16, 2, 16, 128),
        ssem=pltpu.SemaphoreType.DMA((N_SEM,)),
        rsem=pltpu.SemaphoreType.DMA((N_SEM,)),
        lsem=pltpu.SemaphoreType.DMA((N_LOCAL,)),
    )


def finish_kernel(
    out, gin, gmem, o_gu, o_dn, o_b, o_q, o_m, o_small,
    y_out, y_gin, y_gmem, y_g1, y_qkv, y_ao, y_rel, y_g2, y_cq, y_kv, y_co, y_g3, y_gu, y_dn, rel_t,
):
    d = lax.axis_index("dp")
    y_out[...] = out[...]
    y_gin[...] = gin[...]
    y_gmem[...] = gmem[...]
    for half in range(2):
        for q in range(4):
            for c in range(2):
                at = 2048 * half + 512 * q + 256 * c
                y_gu[:, at : at + 256] = o_gu[c, :, 512 * q + 256 * half : 512 * q + 256 * half + 256].astype(f32)
    y_dn[...] = o_dn[...].astype(f32)
    for i, y in enumerate((y_ao, y_cq, y_co)):
        y[...] = o_b[i, 0].astype(f32)
    for p in range(5):
        y, src, i = (y_qkv, o_q, p) if p < 3 else (y_kv, o_m, p - 3)
        for t in range(2):
            two = [src[2 * t + j, :, 192 * i : 192 * i + 192].astype(f32) for j in range(2)]
            y[:, 768 * i + 384 * t : 768 * i + 384 * t + 384] = jnp.concatenate(two, axis=1)
    for i, y in enumerate((y_g1, y_g2, y_g3)):
        line = o_small[12 + i : 13 + i, :]
        val = line[:, 0:192]
        for q in range(1, 4):
            val = jnp.where(d == q, line[:, 192 * q : 192 * q + 192], val)
        y[...] = val
    rel_t[...] = jnp.transpose(o_small[:, 0:128])
    y_rel[...] = rel_t[pl.ds(pl.multiple_of(8 * d, 8), 8), 0:12]


def per_device_kernel(
    inputs, memory, cotangent, segment_ids, row_live, buckets, gain_self, w_qkv, w_attn_out, rel_bias, gain_cross,
    c_query, c_keyval, c_out, gain_ff, w_gate_up, w_down,
):
    anywhere = pl.BlockSpec(memory_space=pl.ANY)
    vmem = pl.BlockSpec(memory_space=pltpu.VMEM)
    smem = pl.BlockSpec(memory_space=pltpu.SMEM)
    shapes = (
        ((2, 128, 768), bf16), ((2, 128, 768), bf16), ((2, 128, 768), bf16),
        ((2, 192, 2048), bf16), ((2, 256, 768), bf16), ((3, 2, 96, 768), bf16), ((4, 192, 576), bf16), ((4, 192, 384), bf16),
        ((16, 768), f32),
    )
    parts = pl.pallas_call(
        layer_kernel,
        out_shape=[jax.ShapeDtypeStruct(*sh) for sh in shapes],
        in_specs=[anywhere] * 3 + [vmem] * 6 + [smem] + [anywhere] * 7,
        out_specs=[anywhere] * 8 + [vmem],
        scratch_shapes=scratch(),
        compiler_params=pltpu.CompilerParams(collective_id=0, has_side_effects=True, vmem_limit_bytes=66500000),
        name="layer",
    )(
        inputs, memory, cotangent, segment_ids, gain_self, gain_cross, gain_ff, rel_bias,
        buckets.reshape(8, 128), row_live, w_qkv, c_keyval, w_attn_out, c_query, c_out, w_gate_up, w_down,
    )
    act = pl.BlockSpec((1, 64, 768), lambda i: (i // 2, i % 2, 0))
    whole = pl.BlockSpec((16, 768), lambda i: (0, 0))

    def rows(n, width):
        return pl.BlockSpec((n, width), lambda i: (i, 0)), jax.ShapeDtypeStruct((4 * n, width), f32)

    line = pl.BlockSpec((1, 192), lambda i: (0, 0)), jax.ShapeDtypeStruct((1, 192), f32)
    square = rows(48, 768)
    tokens = act, jax.ShapeDtypeStruct((2, 128, 768), bf16)
    down = (
        pl.BlockSpec((2, 64, 768), lambda i: (0, i, 0)),
        jax.ShapeDtypeStruct((2, 256, 768), f32),
    )
    table = pl.BlockSpec((8, 12), lambda i: (0, 0)), jax.ShapeDtypeStruct((8, 12), f32)
    outs = (
        tokens, tokens, tokens, line, rows(48, 2304), square, table, line, square, rows(48, 1536), square, line,
        rows(48, 4096), down,
    )
    res = pl.pallas_call(
        finish_kernel,
        grid=(4,),
        out_shape=[o for _, o in outs],
        in_specs=[
            act, act, act,
            pl.BlockSpec((2, 48, 2048), lambda i: (0, i, 0)),
            pl.BlockSpec((2, 64, 768), lambda i: (0, i, 0)),
            pl.BlockSpec((3, 1, 48, 768), lambda i: (0, i // 2, i % 2, 0)),
            pl.BlockSpec((4, 48, 576), lambda i: (0, i, 0)),
            pl.BlockSpec((4, 48, 384), lambda i: (0, i, 0)),
            whole,
        ],
        out_specs=[b for b, _ in outs],
        scratch_shapes=[pltpu.VMEM((128, 16), f32)],
        compiler_params=pltpu.CompilerParams(vmem_limit_bytes=66500000),
        name="finish",
    )(*parts)
    res = list(res)
    for i in (3, 7, 11):
        res[i] = res[i].reshape(192)
    res[13] = res[13].reshape(512, 768)
    return tuple(res)


def solution(mesh):
    in_specs = (
        P("dp", "seq", None),
        P("dp", "seq", None),
        P("dp", "seq", None),
        P("dp", "seq"),
        P("dp"),
        P(),
        P("dp"),
        P("dp", None),
        P("dp", None),
        P("dp", None),
        P("dp"),
        P("dp", None),
        P("dp", None),
        P("dp", None),
        P("dp"),
        P("dp", None),
        P("dp", None),
    )
    out_specs = (
        P("dp", "seq", None),
        P("dp", "seq", None),
        P("dp", "seq", None),
        P("dp"),
        P("dp", None),
        P("dp", None),
        P("dp", None),
        P("dp"),
        P("dp", None),
        P("dp", None),
        P("dp", None),
        P("dp"),
        P("dp", None),
        P("dp", None),
    )
    fits = dict(mesh.shape) == {"dp": 4, "seq": 8}
    return jax.shard_map(
        per_device_kernel if fits else per_device, mesh=mesh, in_specs=in_specs, out_specs=out_specs, check_vma=False
    )
```

profile of v0, /device:TPU:0, one launch (start us, length us, event | category | flops | bytes accessed | tf_op | source)
XLA Modules:
  0.0 227.8 jit_solution(13418134054691994098)
XLA Ops:
  0.7 220.0 %layer.1 = (bf16[2,128,768]{2,1,0:T(8,128)(2,1)}, bf16[2,128,768]{2,1,0:T(8,128)(2,1)}, bf16[2,128,768]{2,1,0:T(8,128)(2,1)}, bf16[2,192,2048]{2,1,0:T(8,128)(2,...) custom-call(bf16[2,128,768]{2,1,0:T(8,128)(2,1)} %x.1, ...), custom_call_target="tpu_custom_call" | custom-call | tf_op jit(solution)/shard_map/layer/pallas_call | solution.py:1375
  220.7 7.0 %finish.1 = (bf16[2,128,768]{2,1,0:T(8,128)(2,1)}, bf16[2,128,768]{2,1,0:T(8,128)(2,1)}, bf16[2,128,768]{2,1,0:T(8,128)(2,1)}, f32[1,192]{1,0:T(1,128)}, f32[192...) custom-call(bf16[2,128,768]{2,1,0:T(8,128)(2,1)} %get-tuple-element., ...), custom_call_target="tpu_custom_call" | custom-call | tf_op jit(solution)/shard_map/finish/pallas_call | solution.py:1405
where the time goes:
time: 232 us; the launch traced here: 228 us
  Pallas kernels  227 us (98%)
    pallas_call x1, Pallas kernels, per_device_kernel(): pl.pallas_call(layer_kernel, out_shape=[jax.ShapeDtypeStruct(*sh) for sh...  220 us
    pallas_call x1, Pallas kernels, per_device_kernel(): pl.pallas_call(finish_kernel, grid=(4,), out_shape=[o for _, o in outs],...  6.98 us

commit v1 on v0

--- a/solution.py
+++ b/solution.py
@@ -757,7 +757,6 @@
     for cp in own_gu:
         cp.wait()
     gu_w = Gather(whole192(wgu), part192(wgu))
-    W3_w[1].relay()
 
     def window(b):
         return pl.ds(pl.multiple_of(b * 256, 256), 768)
@@ -776,6 +775,8 @@
             pack(opack, b, parts)
             a_in.append(push(opack.at[b], arecv.at[g], seqk(k)))
         if k == 2:
+            W3_w[1].relay()
+        if k == 1:
             W3_w[2].relay()
 
     own_dn.wait()
@@ -959,8 +960,13 @@
     f_in = push(fpart, frecv, seqk(1))
     arrived([h_in])
     dv, dgain3 = norm_back(after_cross[...], gains[14:15, :], tbias[c] + hrecv[...].astype(f32))
-    gsm[...] = jnp.zeros((16, 768), f32)
-    gsm[14:15, :] = dgain3
+    gsm[...] = jnp.zeros((32, 128), f32)
+
+    def put_gain(i, val):
+        for j in range(6):
+            gsm[12 + 6 * i + j : 13 + 6 * i + j, :] = val[:, 128 * j : 128 * j + 128]
+
+    put_gain(2, dgain3)
     grad[...] = cotb[c].astype(f32) + dv
     low[0] = (grad[...] * alive).astype(bf16)
     sent(c_in)
@@ -1041,7 +1047,7 @@
     arrived(dq_in)
     assemble(dqrecv, dcq)
     dv, dgain2 = norm_back(after_self[...], gains[13:14, :], dot_nt(dcq[...], W3[1]))
-    gsm[13:14, :] = dgain2
+    put_gain(1, dgain2)
     grad[...] += dv
     sent([h_in])
     low[1] = (grad[...] * alive).astype(bf16)
@@ -1180,11 +1186,11 @@
     mid = rest.astype(bf16)
     last = (rest - mid.astype(f32)).astype(bf16)
     by_bucket = dot_nt(top, hot[...]) + dot_nt(mid, hot[...]) + dot_nt(last, hot[...])
-    row16 = lax.broadcasted_iota(jnp.int32, (16, 128), 0)
-    spot = jnp.zeros((16, 128), f32)
+    row32 = lax.broadcasted_iota(jnp.int32, (32, 128), 0)
+    spot = jnp.zeros((32, 128), f32)
     for h in range(3):
-        spot = jnp.where(row16 == 3 * g + h, jnp.broadcast_to(by_bucket[h : h + 1, :], (16, 128)), spot)
-    gsm[:, 0:128] += spot
+        spot = jnp.where(row32 == 3 * g + h, jnp.broadcast_to(by_bucket[h : h + 1, :], (32, 128)), spot)
+    gsm[...] += spot
 
     for i in (1, 0):
         b_rs[i].end()
@@ -1199,7 +1205,7 @@
     q_far = push(wQ.at[mine], qfar, seqk(4))
 
     dv, dgain1 = norm_back(xown[...], gains[12:13, :], x_rows.total())
-    gsm[12:13, :] = dgain1
+    put_gain(0, dgain1)
     sm_dp = [push(gsm, sm1.at[k - 1], dpk(k)) for k in (1, 2, 3)]
     mem_recv([gmem.at[0], gmem.at[1]])
     mem_sent()
@@ -1319,9 +1325,9 @@
         zb2=vm(bf16, 3, 48, 768),
         qfar=vm(bf16, 192, 576),
         mfar=vm(bf16, 192, 384),
-        gsm=vm(f32, 16, 768),
-        sm1=vm(f32, 3, 16, 768),
-        sm2=vm(f32, 7, 16, 768),
+        gsm=vm(f32, 32, 128),
+        sm1=vm(f32, 3, 32, 128),
+        sm2=vm(f32, 7, 32, 128),
         sgown=vm(bf16, 2, 16, 128),
         ssem=pltpu.SemaphoreType.DMA((N_SEM,)),
         rsem=pltpu.SemaphoreType.DMA((N_SEM,)),
@@ -1351,12 +1357,12 @@
             two = [src[2 * t + j, :, 192 * i : 192 * i + 192].astype(f32) for j in range(2)]
             y[:, 768 * i + 384 * t : 768 * i + 384 * t + 384] = jnp.concatenate(two, axis=1)
     for i, y in enumerate((y_g1, y_g2, y_g3)):
-        line = o_small[12 + i : 13 + i, :]
+        line = jnp.concatenate([o_small[12 + 6 * i + j : 13 + 6 * i + j, :] for j in range(6)], axis=1)
         val = line[:, 0:192]
         for q in range(1, 4):
             val = jnp.where(d == q, line[:, 192 * q : 192 * q + 192], val)
         y[...] = val
-    rel_t[...] = jnp.transpose(o_small[:, 0:128])
+    rel_t[...] = jnp.transpose(o_small[...])
     y_rel[...] = rel_t[pl.ds(pl.multiple_of(8 * d, 8), 8), 0:12]
 
 
@@ -1370,7 +1376,7 @@
     shapes = (
         ((2, 128, 768), bf16), ((2, 128, 768), bf16), ((2, 128, 768), bf16),
         ((2, 192, 2048), bf16), ((2, 256, 768), bf16), ((3, 2, 96, 768), bf16), ((4, 192, 576), bf16), ((4, 192, 384), bf16),
-        ((16, 768), f32),
+        ((32, 128), f32),
     )
     parts = pl.pallas_call(
         layer_kernel,
@@ -1385,7 +1391,7 @@
         buckets.reshape(8, 128), row_live, w_qkv, c_keyval, w_attn_out, c_query, c_out, w_gate_up, w_down,
     )
     act = pl.BlockSpec((1, 64, 768), lambda i: (i // 2, i % 2, 0))
-    whole = pl.BlockSpec((16, 768), lambda i: (0, 0))
+    whole = pl.BlockSpec((32, 128), lambda i: (0, 0))
 
     def rows(n, width):
         return pl.BlockSpec((n, width), lambda i: (i, 0)), jax.ShapeDtypeStruct((4 * n, width), f32)
@@ -1416,7 +1422,7 @@
             whole,
         ],
         out_specs=[b for b, _ in outs],
-        scratch_shapes=[pltpu.VMEM((128, 16), f32)],
+        scratch_shapes=[pltpu.VMEM((128, 32), f32)],
         compiler_params=pltpu.CompilerParams(vmem_limit_bytes=66500000),
         name="finish",
     )(*parts)

time: 232 us -> 227 us (0.978)
  Pallas kernels: 227 us -> 222 us
    pallas_call x1, Pallas kernels: 220 us -> 215 us  [per_device_kernel(): pl.pallas_call(layer_kernel, out_shape=[jax.ShapeDtypeStruct(*sh) for sh...]
where the time goes in v1:
time: 227 us; the launch traced here: 223 us
  Pallas kernels  222 us (98%)
    pallas_call x1, Pallas kernels, per_device_kernel(): pl.pallas_call(layer_kernel, out_shape=[jax.ShapeDtypeStruct(*sh) for sh...  215 us
    pallas_call x1, Pallas kernels, per_device_kernel(): pl.pallas_call(finish_kernel, grid=(4,), out_shape=[o for _, o in outs],...  7.26 us

profile of v1, /device:TPU:0, one launch (start us, length us, event | category | flops | bytes accessed | tf_op | source)
XLA Modules:
  0.0 222.8 jit_solution(326339619337824709)
XLA Ops:
  0.7 214.7 %layer.1 = (bf16[2,128,768]{2,1,0:T(8,128)(2,1)}, bf16[2,128,768]{2,1,0:T(8,128)(2,1)}, bf16[2,128,768]{2,1,0:T(8,128)(2,1)}, bf16[2,192,2048]{2,1,0:T(8,128)(2,...) custom-call(bf16[2,128,768]{2,1,0:T(8,128)(2,1)} %x.1, ...), custom_call_target="tpu_custom_call" | custom-call | tf_op jit(solution)/shard_map/layer/pallas_call | solution.py:1381
  215.3 7.3 %finish.1 = (bf16[2,128,768]{2,1,0:T(8,128)(2,1)}, bf16[2,128,768]{2,1,0:T(8,128)(2,1)}, bf16[2,128,768]{2,1,0:T(8,128)(2,1)}, f32[1,192]{1,0:T(1,128)}, f32[192...) custom-call(bf16[2,128,768]{2,1,0:T(8,128)(2,1)} %get-tuple-element., ...), custom_call_target="tpu_custom_call" | custom-call | tf_op jit(solution)/shard_map/finish/pallas_call | solution.py:1411
